TPU v7x, 32 devices: a whole 2x2x4 slice. The times are simulated.
32 devices in a mesh: blk: 4 (over y, core), cols: 8 (over z, x).
Axes of the slice: x: 2, y: 2, z: 4, core: 2. Of those that a mesh axis runs over, the one named last changes fastest.
Arguments:
- blocks: bfloat16 [8, 16, 24, 128, 128], P('cols', 'blk'), may hold values from -4 to 4
- columns: int32 [8, 16, 24], P('cols', 'blk'), may hold values from 0 to 127, as said below
- counts: int32 [8, 16], P('cols', 'blk'), may hold values from 12 to 24, as said below
- owners: int32 [8, 16, 1], P('cols', 'blk'), may hold values from 0 to 3; in each aligned block of 4 rows (0 to 3, 4 to 7, ..., all dimensions but the last counted through in order) at most 2 rows name the same one
Outputs:
- squared: bfloat16 [8, 4, 8, 24, 128, 128], P('cols', 'blk')
Inputs may be any that keep to these rules, and one draw needn't show every extreme that they name: `columns`: the 24 entries of a block row of slab g are distinct and lie among the 48 block rows of slabs g - 1, g, g + 1, the slab index taken cyclically. `counts`: in every slab some block row has all 24 slots live. `owners`: among the 4 rows of one device each owner appears at most 2 times.
All inputs are finite; a program needn't handle non-finite values.
Results may differ from a plain program's by a relative error of at most 0.001.
Values may be sent and summed in bfloat16 or wider, within the bound.
A program may use at most 192 MiB of HBM per device.

v0:
```python
import functools

import jax
import jax.numpy as jnp
from jax import lax
from jax.experimental import pallas as pl
from jax.experimental.pallas import tpu as pltpu
from jax.sharding import PartitionSpec as P

CAP = 2
DEPTH = 8
TOGETHER = 4
SHIFT = 12
ROWS, LANES = 8, 128
SPLIT = 1
WINDOW = 2
CYCLE = 2
VIA_PAIR = 1
VIA_FAR = 1
MESH = pl.DeviceIdType.MESH

OWN, PAIR, FAR = 0, 1, 2


def gather_kernel(
    ngroups, rows_dev, blocks_ref, meta_ref, panel_ref, near_ref, send_sem, recv_sem, own_sem
):
    g = lax.axis_index("cols")
    j = lax.axis_index("blk")
    odd = g % 2
    core = j % 2
    side = j // 2
    pair = g + 1 - 2 * odd
    ahead = (g + 2 - 4 * odd + ngroups) % ngroups
    behind = (g - 2 + 4 * odd + ngroups) % ngroups
    slab = {OWN: 1, PAIR: 2 - 2 * odd, FAR: 2 * odd}
    member = {
        0: j,
        1: side * 2 + 1 - core,
        2: (1 - side) * 2 + core,
        3: (1 - side) * 2 + 1 - core,
    }
    device = {
        "core": (g, member[1]),
        "side": (g, member[2]),
        "pair": (pair, j),
        "ahead": (ahead, j),
    }

    barrier = pltpu.get_barrier_semaphore()
    partners = list(device.values()) + [(behind, j)]
    for to_g, to_j in partners:
        pl.semaphore_signal(
            barrier, inc=1, device_id={"cols": to_g, "blk": to_j}, device_id_type=MESH
        )
    pl.semaphore_wait(barrier, len(partners))

    pending = []

    def place(kind, who, m):
        if m == rows_dev:
            return near_ref.at[slab[kind], member[who]]
        return panel_ref.at[slab[kind], member[who] * rows_dev + m]

    def copy(kind, who, m, to, there_kind, there_who):
        slab_there = slab[FAR] if to in ("pair", "ahead") else slab[kind]
        if m == rows_dev:
            mine, there = meta_ref, near_ref.at[slab_there, member[who]]
        else:
            mine = blocks_ref.at[0, m]
            there = panel_ref.at[slab_there, member[who] * rows_dev + m]
        src = mine if (kind, who) == (OWN, 0) else place(kind, who, m)
        to_g, to_j = device[to]
        made = pltpu.make_async_remote_copy(
            src_ref=src,
            dst_ref=there,
            send_sem=send_sem.at[there_kind, there_who, m],
            recv_sem=recv_sem.at[there_kind, there_who, m],
            device_id={"cols": to_g, "blk": to_j},
            device_id_type=MESH,
        )
        made.start()
        pending.append(made)

    def arrived(kind, who, m):
        pltpu.make_async_copy(
            place(kind, who, m), place(kind, who, m), recv_sem.at[kind, who, m]
        ).wait()

    order = [rows_dev] + list(range(rows_dev))
    later = list(order)

    def launch():
        if later:
            m = later.pop(0)
            copy(OWN, 0, m, "pair", PAIR, 0)
            copy(OWN, 0, m, "side", OWN, 2)
            copy(OWN, 0, m, "core", OWN, 1)

    for _ in range(WINDOW + 1):
        launch()
    local_copies = [
        pltpu.make_async_copy(
            blocks_ref.at[0], panel_ref.at[1, pl.ds(j * rows_dev, rows_dev)], own_sem.at[0]
        ),
        pltpu.make_async_copy(meta_ref, near_ref.at[1, j], own_sem.at[1]),
    ]
    for made in local_copies:
        made.start()

    def first(m):
        arrived(PAIR, 0, m)
        copy(PAIR, 0, m, "ahead", FAR, 0)
        if m % CYCLE >= VIA_PAIR:
            copy(PAIR, 0, m, "side", PAIR, 2)
        copy(PAIR, 0, m, "core", PAIR, 1)
        arrived(OWN, 2, m)
        if m % CYCLE < VIA_PAIR:
            copy(OWN, 2, m, "pair", PAIR, 2)
        copy(OWN, 2, m, "core", OWN, 3)
        if m != rows_dev:
            launch()

    def second(m):
        arrived(FAR, 0, m)
        if m % CYCLE >= VIA_FAR:
            copy(FAR, 0, m, "side", FAR, 2)
        copy(FAR, 0, m, "core", FAR, 1)
        arrived(PAIR, 2, m)
        if m % CYCLE < VIA_FAR:
            copy(PAIR, 2, m, "ahead", FAR, 2)
        copy(PAIR, 2, m, "core", PAIR, 3)

    def third(m):
        arrived(FAR, 2, m)
        copy(FAR, 2, m, "core", FAR, 3)

    for step in range(len(order) + 2):
        for back, stage in enumerate((first, second, third)):
            if 0 <= step - back < len(order):
                stage(order[step - back])
    for kind in (OWN, PAIR, FAR):
        for who in (1, 3):
            for m in order:
                arrived(kind, who, m)
    for made in pending:
        made.wait_send()
    for made in local_copies:
        made.wait()


def gather_panel(blocks, meta, ngroups, group_rows):
    rows_dev, stored, width = blocks.shape[1:4]
    return pl.pallas_call(
        functools.partial(gather_kernel, ngroups, rows_dev),
        out_shape=(
            jax.ShapeDtypeStruct((3, group_rows, stored, width, width), blocks.dtype),
            jax.ShapeDtypeStruct((3, group_rows // rows_dev) + meta.shape, meta.dtype),
        ),
        in_specs=[pl.BlockSpec(memory_space=pl.ANY)] * 2,
        out_specs=[pl.BlockSpec(memory_space=pl.ANY)] * 2,
        scratch_shapes=[
            pltpu.SemaphoreType.DMA((3, 4, rows_dev + 1)),
            pltpu.SemaphoreType.DMA((3, 4, rows_dev + 1)),
            pltpu.SemaphoreType.DMA((2,)),
        ],
        compiler_params=pltpu.CompilerParams(collective_id=0, has_side_effects=True),
        name="gather_panel",
    )(blocks, meta)


def exact_dot(left, right, dims=((1,), (0,))):
    return lax.dot_general(
        left.astype(jnp.bfloat16),
        right.astype(jnp.bfloat16),
        (dims, ((), ())),
        preferred_element_type=jnp.float32,
    )


def work_lists(meta, me, offset, total_rows, rows_dev, stored, nblk):
    held = meta.shape[0]
    window = 3 * nblk * rows_dev
    results = nblk * CAP * stored
    bits = ROWS.bit_length() - 1

    def iota(shape, axis):
        return lax.broadcasted_iota(jnp.int32, shape, axis)

    row = iota((results, 1), 0)
    slot = jnp.zeros_like(row)
    for k in range(1, nblk * CAP):
        slot += (row >= k * stored).astype(jnp.int32)
    source = jnp.zeros_like(row)
    for k in range(1, nblk):
        source += (slot >= k * CAP).astype(jnp.int32)
    turn = slot - CAP * source
    item = row - slot * stored
    lane = iota((results, LANES), 1)
    at = iota((results, held), 1)
    shard = at >> bits
    within = at & (ROWS - 1)
    index = shard * rows_dev + within

    picks = (lane == stored).astype(jnp.float32)
    owner = exact_dot(picks, meta.astype(jnp.float32), ((1,), (1,)))
    mine = (owner == me.astype(jnp.float32)) & (within < rows_dev) & (shard == source + nblk)
    mine = mine.astype(jnp.float32)
    before = (iota((held, held), 0) < iota((held, held), 1)).astype(jnp.float32)
    rank = exact_dot(mine, before)
    chosen = jnp.where(rank == turn.astype(jnp.float32), mine, 0.0)

    far = meta - offset
    far = jnp.where(far < 0, far + total_rows, far)
    far = jnp.where(far >= total_rows, far - total_rows, far)
    live = (meta >= 0) & (far < window) & (iota(meta.shape, 1) < stored)
    near = jnp.where(live, far + 1, 0).astype(jnp.float32)

    left = exact_dot(chosen, near)
    partner = jnp.sum(jnp.where(lane == item, left, 0.0), axis=1, keepdims=True)
    partner = partner.astype(jnp.int32) - 1
    right = exact_dot(((index == partner) & (within < rows_dev)).astype(jnp.float32), near)
    found = jnp.full((results, LANES), -1, jnp.int32)
    for i in range(stored):
        found = jnp.where((right == left[:, i : i + 1]) & (right > 0), i, found)
    match = found >= 0
    ahead = (iota((LANES, LANES), 0) < iota((LANES, LANES), 1)).astype(jnp.float32)
    place = exact_dot(match.astype(jnp.float32), ahead).astype(jnp.int32)
    place = jnp.where(match, place, -1)
    left_row = jnp.sum(chosen * index.astype(jnp.float32), axis=1, keepdims=True)
    code = left_row.astype(jnp.int32) * stored + found
    code += (partner * stored + lane) << SHIFT
    pairs = jnp.full((results, LANES), window * stored, jnp.int32)
    for u in range(stored):
        pairs = jnp.where(place[:, u : u + 1] == lane, code[:, u : u + 1], pairs)
    count = jnp.sum(match.astype(jnp.float32), axis=1, keepdims=True).astype(jnp.int32)
    return jnp.where(lane == LANES - 1, count, pairs)


def product_kernel(
    dims, near_ref, panel_hbm, out_ref, panel, lists, pairs_ref, sem, list_sem
):
    nblk, ngroups, rows_dev, stored = dims
    slot = pl.program_id(0)
    width = panel.shape[1]
    total = panel_hbm.shape[0]

    @pl.when(slot == 0)
    def _():
        fetch = pltpu.make_async_copy(panel_hbm, panel.at[pl.ds(0, total)], sem)
        fetch.start()
        panel[total] = jnp.zeros((width, width), panel.dtype)
        group_rows = nblk * rows_dev
        lists[...] = work_lists(
            near_ref[...],
            lax.axis_index("blk"),
            (lax.axis_index("cols") - 1) * group_rows,
            ngroups * group_rows,
            rows_dev,
            stored,
            nblk,
        )
        send = pltpu.make_async_copy(lists, pairs_ref, list_sem)
        send.start()
        send.wait()
        fetch.wait()

    bunches = stored // TOGETHER

    def one_bunch(bunch, carry):
        first = bunch * TOGETHER
        most = 0
        for n in range(TOGETHER):
            most = jnp.maximum(most, pairs_ref[slot * stored + first + n, LANES - 1])

        def step(trip, sums):
            new = []
            for n in range(TOGETHER):
                lefts, rights = [], []
                for d in range(DEPTH):
                    code = pairs_ref[slot * stored + first + n, trip * DEPTH + d]
                    lefts.append(panel[code & ((1 << SHIFT) - 1)])
                    rights.append(panel[code >> SHIFT])
                new.append(
                    sums[n]
                    + lax.dot_general(
                        jnp.concatenate(lefts, axis=1),
                        jnp.concatenate(rights, axis=1),
                        (((1,), (1,)), ((), ())),
                        preferred_element_type=jnp.float32,
                    )
                )
            return tuple(new)

        zero = jnp.zeros((width, width), jnp.float32)
        trips = (most + DEPTH - 1) // DEPTH
        sums = lax.fori_loop(0, trips, step, (zero,) * TOGETHER)
        for n in range(TOGETHER):
            out_ref[0, 0, 0, first + n] = sums[n].astype(out_ref.dtype)
        return carry

    lax.fori_loop(0, bunches, one_bunch, 0)


def products(panel, near, nblk, ngroups, rows_dev, stored):
    total, width = panel.shape[0], panel.shape[1]
    slots = nblk * CAP
    return pl.pallas_call(
        functools.partial(product_kernel, (nblk, ngroups, rows_dev, stored)),
        out_shape=jax.ShapeDtypeStruct((1, 1, slots, stored, width, width), panel.dtype),
        grid=(slots,),
        in_specs=[
            pl.BlockSpec(near.shape, lambda slot: (0, 0)),
            pl.BlockSpec(memory_space=pl.ANY),
        ],
        out_specs=pl.BlockSpec(
            (1, 1, 1, stored, width, width), lambda slot: (0, 0, slot, 0, 0, 0)
        ),
        scratch_shapes=[
            pltpu.VMEM((total + 1, width, width), panel.dtype),
            pltpu.VMEM((slots * stored, LANES), jnp.int32),
            pltpu.SMEM((slots * stored, LANES), jnp.int32),
            pltpu.SemaphoreType.DMA,
            pltpu.SemaphoreType.DMA,
        ],
        compiler_params=pltpu.CompilerParams(vmem_limit_bytes=50 * 1024 * 1024),
        name="products",
    )(near, panel)


def local(blocks, columns, counts, owners, *, nblk, ngroups):
    rows_dev, stored, width = blocks.shape[1:4]
    group_rows = nblk * rows_dev
    slot_iota = jnp.arange(stored, dtype=jnp.int32)
    marked = jnp.where(slot_iota[None, None, :] < counts[:, :, None], columns, -1)
    meta = jnp.concatenate([marked[0], owners[0]], axis=1)
    meta = jnp.pad(
        meta, ((0, ROWS - rows_dev), (0, LANES - stored - 1)), constant_values=-1
    )
    pieces = blocks.reshape(1, rows_dev * SPLIT, stored // SPLIT, width, width)
    panel, near = gather_panel(pieces, meta, ngroups, group_rows * SPLIT)
    panel = panel.reshape(3 * group_rows * stored, width, width)
    near = near.reshape(3 * nblk * ROWS, LANES)
    return products(panel, near, nblk, ngroups, rows_dev, stored)


def solution(mesh):
    placed = (
        P("cols", "blk", None, None, None),
        P("cols", "blk", None),
        P("cols", "blk"),
        P("cols", "blk", None),
    )
    return jax.shard_map(
        functools.partial(local, nblk=mesh.shape["blk"], ngroups=mesh.shape["cols"]),
        mesh=mesh,
        in_specs=placed,
        out_specs=P("cols", "blk", None, None, None, None),
        check_vma=False,
    )
```

profile of v0, /device:TPU:0, one launch (start us, length us, event | category | flops | bytes accessed | tf_op | source)
XLA Modules:
  0.0 182.3 jit_solution(6318735217980014854)
XLA Ops:
  0.0 0.8 select_bitcast_fusion
  0.8 0.7 copy.5
  1.5 0.1 pad_add_fusion
  1.6 0.6 pad.4.meta_ref
  2.2 145.6 %gather_panel.1 = (bf16[3,16,24,128,128]{4,3,2,1,0:T(8,128)(2,1)}, s32[3,4,8,128]{3,2,1,0:T(8,128)}) custom-call(bf16[1,4,24,128,128]{4,3,2,1,0:T(8,128)(2,1)} %blocks_ref.1, s32[8,128]{1,0:T(8,128)} %pad.4.meta_ref), custom_call_target="tpu_custom_call" | custom-call | tf_op jit(solution)/shard_map/gather_panel/pallas_call | solution.py:154
  147.8 0.0 copy-start
  147.8 0.8 copy-done
  148.6 33.8 %products.1 = bf16[1,1,8,24,128,128]{5,4,3,2,1,0:T(8,128)(2,1)} custom-call(s32[96,128]{1,0:T(8,128)S(1)} %bitcast.6, bf16[1152,128,128]{2,1,0:T(8,128)(2,1)} %bitcast.7), custom_call_target="tpu_custom_call" | custom-call | tf_op jit(solution)/shard_map/products/pallas_call | solution.py:308
Async XLA Ops:
  147.8 0.8 copy-start
where the time goes:
time: 184 us; the launch traced here: 182 us
  Pallas kernels  179 us (97%)
  local copies, waits for them, and re-layouts  2.13 us (1%)
    pallas_call x1, Pallas kernels, gather_panel(): pl.pallas_call(functools.partial(gather_kernel, ngroups, rows_dev), out_s...  146 us
    pallas_call x1, Pallas kernels, products(): pl.pallas_call(functools.partial(product_kernel, (nblk, ngroups, rows_dev...  33.8 us

commit v1 on v0

--- a/solution.py
+++ b/solution.py
@@ -8,7 +8,7 @@
 from jax.sharding import PartitionSpec as P
 
 CAP = 2
-DEPTH = 8
+DEPTH = 12
 TOGETHER = 4
 SHIFT = 12
 ROWS, LANES = 8, 128

time: 184 us -> 184 us (level)
  no operation moved by 1% of the time
where the time goes in v1:
time: 184 us; the launch traced here: 183 us
  Pallas kernels  180 us (98%)
  local copies, waits for them, and re-layouts  2.13 us (1%)
    pallas_call x1, Pallas kernels, gather_panel(): pl.pallas_call(functools.partial(gather_kernel, ngroups, rows_dev), out_s...  146 us
    pallas_call x1, Pallas kernels, products(): pl.pallas_call(functools.partial(product_kernel, (nblk, ngroups, rows_dev...  34.1 us

profile of v1, /device:TPU:0, one launch (start us, length us, event | category | flops | bytes accessed | tf_op | source)
XLA Modules:
  0.0 182.6 jit_solution(349658139857734751)
XLA Ops:
  0.0 0.8 select_bitcast_fusion
  0.8 0.7 copy.5
  1.5 0.1 pad_add_fusion
  1.6 0.6 pad.4.meta_ref
  2.2 145.6 %gather_panel.1 = (bf16[3,16,24,128,128]{4,3,2,1,0:T(8,128)(2,1)}, s32[3,4,8,128]{3,2,1,0:T(8,128)}) custom-call(bf16[1,4,24,128,128]{4,3,2,1,0:T(8,128)(2,1)} %blocks_ref.1, s32[8,128]{1,0:T(8,128)} %pad.4.meta_ref), custom_call_target="tpu_custom_call" | custom-call | tf_op jit(solution)/shard_map/gather_panel/pallas_call | solution.py:154
  147.8 0.0 copy-start
  147.8 0.8 copy-done
  148.6 34.1 %products.1 = bf16[1,1,8,24,128,128]{5,4,3,2,1,0:T(8,128)(2,1)} custom-call(s32[96,128]{1,0:T(8,128)S(1)} %bitcast.6, bf16[1152,128,128]{2,1,0:T(8,128)(2,1)} %bitcast.7), custom_call_target="tpu_custom_call" | custom-call | tf_op jit(solution)/shard_map/products/pallas_call | solution.py:308
Async XLA Ops:
  147.8 0.8 copy-start
